TPU v7x, 32 devices: a whole 2x2x4 slice. The times are simulated.
32 devices in a mesh: gx: 2 (over y), gy: 4 (over x, core), gz: 4 (over z).
Axes of the slice: x: 2, y: 2, z: 4, core: 2. Of those that a mesh axis runs over, the one named last changes fastest.
Arguments:
- right_side: float32 [16, 128, 1024], P('gx', 'gy', 'gz'), may hold values from -60 to 60
- wavenumber_sq: float32 [16, 128, 1024], P('gx', 'gy', 'gz'), may hold values from 0.3 to 1.5
- sketch_matrix: float32 [16, 16, 128, 1024], P(None, 'gx', 'gy', 'gz'), may hold values from -1.5 to 1.5
Outputs:
- solution: float32 [16, 128, 1024], P('gx', 'gy', 'gz')
- residual: float32 [16, 128, 1024], P('gx', 'gy', 'gz')
All inputs are finite; a program needn't handle non-finite values.
Results may differ from a plain program's by a relative error of at most 0.0003.
Values sent between devices are 32-bit elements; how exact they have to be, the bound alone decides.
A program may use at most 64 MiB of HBM per device.

v0:
```python
import jax
import jax.numpy as jnp
from jax import lax
from jax.sharding import PartitionSpec as P

SWEEPS = 3
ITERS = 3


HIGH = lax.Precision.HIGHEST


def extended(block, sides, width):
    for axis, dim in sides:
        count = lax.axis_size(axis)
        forward = [(i, i + 1) for i in range(count - 1)]
        forward.append((count - 1, 0))
        backward = [(target, source) for source, target in forward]
        low = lax.ppermute(
            lax.slice_in_dim(block, block.shape[dim] - width, None, axis=dim), axis, forward
        )
        high = lax.ppermute(lax.slice_in_dim(block, 0, width, axis=dim), axis, backward)
        block = jnp.concatenate([low, block, high], axis=dim)
    return block


def stencil_near(padded):
    total = padded[2:, 1:-1, 1:-1] + padded[:-2, 1:-1, 1:-1]
    total = total + padded[1:-1, 2:, 1:-1] + padded[1:-1, :-2, 1:-1]
    total = total + padded[1:-1, 1:-1, 2:] + padded[1:-1, 1:-1, :-2]
    return total


def with_faces(grid_field):
    return extended(grid_field, (("gx", 0), ("gy", 1), ("gz", 2)), 1)


def shallow_apply(vector, wavenumber_sq):
    diagonal = 6.0 + wavenumber_sq
    result = vector / diagonal
    for sweep_idx in range(SWEEPS):
        result = (
            result + (vector - (diagonal * result - stencil_near(with_faces(result)))) / diagonal
        )
    product = (6.0 - wavenumber_sq) * result - stencil_near(with_faces(result))
    return (result, product)


def local_sketch(sketch_rows, grid_field):
    return jnp.dot(
        sketch_rows, grid_field.reshape(-1), precision=HIGH, preferred_element_type=jnp.float32
    )


def solve_small(hessen, beta_norm):
    target = jnp.zeros((ITERS + 1,), jnp.float32).at[0].set(beta_norm)
    basis = []
    upper = [[None] * ITERS for row_idx in range(ITERS)]
    for col_idx in range(ITERS):
        column = hessen[:, col_idx]
        for row_idx in range(col_idx):
            factor = jnp.sum(basis[row_idx] * column)
            upper[row_idx][col_idx] = factor
            column = column - factor * basis[row_idx]
        diag_term = jnp.sqrt(jnp.sum(column * column))
        upper[col_idx][col_idx] = diag_term
        basis.append(column / diag_term)
    projected = [jnp.sum(member * target) for member in basis]
    coeffs = [None] * ITERS
    for row_idx in reversed(range(ITERS)):
        accum = projected[row_idx]
        for col_idx in range(row_idx + 1, ITERS):
            accum = accum - upper[row_idx][col_idx] * coeffs[col_idx]
        coeffs[row_idx] = accum / upper[row_idx][row_idx]
    weights = jnp.stack(coeffs)
    leftover = target - jnp.dot(hessen, weights, precision=HIGH)
    return (weights, leftover)


def local(right_side, wavenumber_sq, sketch_matrix):
    sketch_rows = sketch_matrix.reshape(sketch_matrix.shape[0], -1)
    rhs_sketch = lax.psum(local_sketch(sketch_rows, right_side), ("gx", "gy", "gz"))
    beta_norm = jnp.sqrt(jnp.sum(rhs_sketch * rhs_sketch))
    vectors = [right_side / beta_norm]
    images = [rhs_sketch / beta_norm]
    directions = []
    hessen = jnp.zeros((ITERS + 1, ITERS), jnp.float32)
    for iteration in range(ITERS):
        direction, product = shallow_apply(vectors[-1], wavenumber_sq)
        directions.append(direction)
        sketch_new = lax.psum(local_sketch(sketch_rows, product), ("gx", "gy", "gz"))
        stacked = jnp.stack(images, axis=1)
        weights = jnp.dot(sketch_new, stacked, precision=HIGH)
        remainder = product
        for member in range(iteration + 1):
            remainder = remainder - weights[member] * vectors[member]
        sketch_rem = sketch_new - jnp.dot(stacked, weights, precision=HIGH)
        length = jnp.sqrt(jnp.sum(sketch_rem * sketch_rem))
        vectors.append(remainder / length)
        images.append(sketch_rem / length)
        hessen = hessen.at[: iteration + 1, iteration].set(weights)
        hessen = hessen.at[iteration + 1, iteration].set(length)
    coeffs, leftover = solve_small(hessen, beta_norm)
    solution = directions[0] * coeffs[0]
    for member in range(1, ITERS):
        solution = solution + directions[member] * coeffs[member]
    residual = vectors[0] * leftover[0]
    for member in range(1, ITERS + 1):
        residual = residual + vectors[member] * leftover[member]
    return (solution, residual)


def solution(mesh):
    return jax.shard_map(
        local,
        mesh=mesh,
        in_specs=(P("gx", "gy", "gz"), P("gx", "gy", "gz"), P(None, "gx", "gy", "gz")),
        out_specs=(P("gx", "gy", "gz"), P("gx", "gy", "gz")),
        check_vma=False,
    )
```

profile of v0, /device:TPU:0, one launch (start us, length us, event | category | flops | bytes accessed | tf_op | source)
XLA Modules:
  0.0 493.6 jit_solution(14192034118906096870)
XLA Ops:
  0.6 8.8 %fusion.8 = f32[16]{0:T(128)S(1)} fusion(f32[16,8,32,256]{3,2,1,0:T(8,128)} %param.19, f32[8,32,256,1]{2,1,0,3:T(8,128)} %bitcast.124), kind=kOutput, calls=%fused_computation.10 | convolution fusion | flops 12582912 | bytes 4456512 | tf_op jit(solution)/shard_map/dot_general | solution.py:50
  9.5 42.0 %psum.28 = f32[16]{0:T(128)S(1)} all-reduce(f32[16]{0:T(128)S(1)} %fusion.8), channel_id=1, replica_groups=mesh['gx'=2,'gy'=4,'gz'=4] {'gx','gy','gz'}, use_global_device_ids=true, to_apply=%region_0.0 | all-reduce | flops 16 | bytes 128 | tf_op jit(solution)/shard_map/psum | solution.py:82
  52.8 2.3 collective-permute-start.1
  57.1 2.0 collective-permute-done
  62.4 2.2 collective-permute-start.4
  64.7 5.5 %collective-permute-done.4 = f32[10,34,1]{2,1,0:T(8,128)S(1)} collective-permute-done((f32[10,34,1]{2,1,0:T(8,128)S(1)}, f32[10,34,1]{2,1,0:T(8,128)S(1)}, u32[]{:S(2)}, u32[]{:S(2)}) %collective-permute-start.4) | collective-permute-done | bytes 1392 | tf_op jit(solution)/shard_map/ppermute | solution.py:22
  70.2 6.1 %collective-permute-done.5 = f32[10,34,1]{2,1,0:T(8,128)S(1)} collective-permute-done((f32[10,34,1]{2,1,0:T(8,128)S(1)}, f32[10,34,1]{2,1,0:T(8,128)S(1)}, u32[]{:S(2)}, u32[]{:S(2)}) %collective-permute-start.5) | collective-permute-done | bytes 1392 | tf_op jit(solution)/shard_map/ppermute | solution.py:19
  76.7 2.0 collective-permute-start.6
  78.7 1.9 collective-permute-done.7
  84.3 2.1 collective-permute-start.10
  86.4 5.3 %collective-permute-done.10 = f32[10,34,1]{2,1,0:T(8,128)S(1)} collective-permute-done((f32[10,34,1]{2,1,0:T(8,128)S(1)}, f32[10,34,1]{2,1,0:T(8,128)S(1)}, u32[]{:S(2)}, u32[]{:S(2)}) %collective-permute-start.10) | collective-permute-done | bytes 1392 | tf_op jit(solution)/shard_map/ppermute | solution.py:22
  91.8 5.5 %collective-permute-done.11 = f32[10,34,1]{2,1,0:T(8,128)S(1)} collective-permute-done((f32[10,34,1]{2,1,0:T(8,128)S(1)}, f32[10,34,1]{2,1,0:T(8,128)S(1)}, u32[]{:S(2)}, u32[]{:S(2)}) %collective-permute-start.11) | collective-permute-done | bytes 1392 | tf_op jit(solution)/shard_map/ppermute | solution.py:19
  99.7 1.9 collective-permute-done.13
  106.4 1.9 collective-permute-start.16
  108.5 5.8 %collective-permute-done.16 = f32[10,34,1]{2,1,0:T(8,128)S(1)} collective-permute-done((f32[10,34,1]{2,1,0:T(8,128)S(1)}, f32[10,34,1]{2,1,0:T(8,128)S(1)}, u32[]{:S(2)}, u32[]{:S(2)}) %collective-permute-start.16) | collective-permute-done | bytes 1392 | tf_op jit(solution)/shard_map/ppermute | solution.py:22
  114.3 4.8 collective-permute-done.17
  121.6 1.9 collective-permute-done.19
  127.4 2.1 collective-permute-start.22
  129.7 5.2 %collective-permute-done.22 = f32[10,34,1]{2,1,0:T(8,128)S(1)} collective-permute-done((f32[10,34,1]{2,1,0:T(8,128)S(1)}, f32[10,34,1]{2,1,0:T(8,128)S(1)}, u32[]{:S(2)}, u32[]{:S(2)}) %collective-permute-start.22) | collective-permute-done | bytes 1392 | tf_op jit(solution)/shard_map/ppermute | solution.py:22
  134.9 6.1 %collective-permute-done.23 = f32[10,34,1]{2,1,0:T(8,128)S(1)} collective-permute-done((f32[10,34,1]{2,1,0:T(8,128)S(1)}, f32[10,34,1]{2,1,0:T(8,128)S(1)}, u32[]{:S(2)}, u32[]{:S(2)}) %collective-permute-start.23) | collective-permute-done | bytes 1392 | tf_op jit(solution)/shard_map/ppermute | solution.py:19
  141.4 6.9 %fusion.11 = f32[16]{0:T(128)S(1)} fusion(f32[16,8,32,256]{3,2,1,0:T(8,128)S(1)} %copy-done, f32[8,32,256,1]{2,1,0,3:T(8,128)S(1)} %bitcast.125), kind=kOutput, calls=%fused_computation.11 | convolution fusion | flops 12582912 | bytes 4456512 | tf_op jit(solution)/shard_map/dot_general | solution.py:50
  148.3 38.6 %psum.29 = f32[16]{0:T(128)S(1)} all-reduce(f32[16]{0:T(128)S(1)} %fusion.11), channel_id=1, replica_groups=mesh['gx'=2,'gy'=4,'gz'=4] {'gx','gy','gz'}, use_global_device_ids=true, to_apply=%region_2.0 | all-reduce | flops 16 | bytes 128 | tf_op jit(solution)/shard_map/psum | solution.py:91
  190.2 2.3 collective-permute-start.25
  194.4 2.0 collective-permute-done.24
  199.8 2.3 collective-permute-start.28
  202.1 5.5 %collective-permute-done.28 = f32[10,34,1]{2,1,0:T(8,128)S(1)} collective-permute-done((f32[10,34,1]{2,1,0:T(8,128)S(1)}, f32[10,34,1]{2,1,0:T(8,128)S(1)}, u32[]{:S(2)}, u32[]{:S(2)}) %collective-permute-start.28) | collective-permute-done | bytes 1392 | tf_op jit(solution)/shard_map/ppermute | solution.py:22
  207.6 6.0 %collective-permute-done.29 = f32[10,34,1]{2,1,0:T(8,128)S(1)} collective-permute-done((f32[10,34,1]{2,1,0:T(8,128)S(1)}, f32[10,34,1]{2,1,0:T(8,128)S(1)}, u32[]{:S(2)}, u32[]{:S(2)}) %collective-permute-start.29) | collective-permute-done | bytes 1392 | tf_op jit(solution)/shard_map/ppermute | solution.py:19
  214.7 2.0 collective-permute-start.30
  216.7 1.9 collective-permute-done.31
  222.3 2.1 collective-permute-start.34
  224.4 5.6 %collective-permute-done.34 = f32[10,34,1]{2,1,0:T(8,128)S(1)} collective-permute-done((f32[10,34,1]{2,1,0:T(8,128)S(1)}, f32[10,34,1]{2,1,0:T(8,128)S(1)}, u32[]{:S(2)}, u32[]{:S(2)}) %collective-permute-start.34) | collective-permute-done | bytes 1392 | tf_op jit(solution)/shard_map/ppermute | solution.py:22
  230.0 5.3 %collective-permute-done.35 = f32[10,34,1]{2,1,0:T(8,128)S(1)} collective-permute-done((f32[10,34,1]{2,1,0:T(8,128)S(1)}, f32[10,34,1]{2,1,0:T(8,128)S(1)}, u32[]{:S(2)}, u32[]{:S(2)}) %collective-permute-start.35) | collective-permute-done | bytes 1392 | tf_op jit(solution)/shard_map/ppermute | solution.py:19
  237.7 1.9 collective-permute-done.37
  244.7 2.1 collective-permute-start.40
  246.8 5.7 %collective-permute-done.40 = f32[10,34,1]{2,1,0:T(8,128)S(1)} collective-permute-done((f32[10,34,1]{2,1,0:T(8,128)S(1)}, f32[10,34,1]{2,1,0:T(8,128)S(1)}, u32[]{:S(2)}, u32[]{:S(2)}) %collective-permute-start.40) | collective-permute-done | bytes 1392 | tf_op jit(solution)/shard_map/ppermute | solution.py:22
  252.4 5.5 %collective-permute-done.41 = f32[10,34,1]{2,1,0:T(8,128)S(1)} collective-permute-done((f32[10,34,1]{2,1,0:T(8,128)S(1)}, f32[10,34,1]{2,1,0:T(8,128)S(1)}, u32[]{:S(2)}, u32[]{:S(2)}) %collective-permute-start.41) | collective-permute-done | bytes 1392 | tf_op jit(solution)/shard_map/ppermute | solution.py:19
  260.3 1.9 collective-permute-done.43
  266.0 2.0 collective-permute-start.46
  269.5 4.4 collective-permute-done.46
  273.9 5.5 %collective-permute-done.47 = f32[10,34,1]{2,1,0:T(8,128)S(1)} collective-permute-done((f32[10,34,1]{2,1,0:T(8,128)S(1)}, f32[10,34,1]{2,1,0:T(8,128)S(1)}, u32[]{:S(2)}, u32[]{:S(2)}) %collective-permute-start.47) | collective-permute-done | bytes 1392 | tf_op jit(solution)/shard_map/ppermute | solution.py:19
  279.8 6.9 %fusion.14 = f32[16]{0:T(128)S(1)} fusion(f32[16,8,32,256]{3,2,1,0:T(8,128)S(1)} %copy-done.1, f32[8,32,256,1]{2,1,0,3:T(8,128)S(1)} %bitcast.127), kind=kOutput, calls=%fused_computation.12 | convolution fusion | flops 12582912 | bytes 4456512 | tf_op jit(solution)/shard_map/dot_general | solution.py:50
  286.8 39.2 %psum.30 = f32[16]{0:T(128)S(1)} all-reduce(f32[16]{0:T(128)S(1)} %fusion.14), channel_id=1, replica_groups=mesh['gx'=2,'gy'=4,'gz'=4] {'gx','gy','gz'}, use_global_device_ids=true, to_apply=%region_5.0 | all-reduce | flops 16 | bytes 128 | tf_op jit(solution)/shard_map/psum | solution.py:91
  326.0 1.9 broadcast_select_fusion.1
  331.5 2.3 collective-permute-start.49
  335.7 2.0 collective-permute-done.48
  341.1 2.3 collective-permute-start.52
  343.4 5.7 %collective-permute-done.52 = f32[10,34,1]{2,1,0:T(8,128)S(1)} collective-permute-done((f32[10,34,1]{2,1,0:T(8,128)S(1)}, f32[10,34,1]{2,1,0:T(8,128)S(1)}, u32[]{:S(2)}, u32[]{:S(2)}) %collective-permute-start.52) | collective-permute-done | bytes 1392 | tf_op jit(solution)/shard_map/ppermute | solution.py:22
  349.1 5.6 %collective-permute-done.53 = f32[10,34,1]{2,1,0:T(8,128)S(1)} collective-permute-done((f32[10,34,1]{2,1,0:T(8,128)S(1)}, f32[10,34,1]{2,1,0:T(8,128)S(1)}, u32[]{:S(2)}, u32[]{:S(2)}) %collective-permute-start.53) | collective-permute-done | bytes 1392 | tf_op jit(solution)/shard_map/ppermute | solution.py:19
  355.1 2.0 collective-permute-start.54
  357.1 1.9 collective-permute-done.55
  362.8 2.1 collective-permute-start.58
  364.8 5.6 %collective-permute-done.58 = f32[10,34,1]{2,1,0:T(8,128)S(1)} collective-permute-done((f32[10,34,1]{2,1,0:T(8,128)S(1)}, f32[10,34,1]{2,1,0:T(8,128)S(1)}, u32[]{:S(2)}, u32[]{:S(2)}) %collective-permute-start.58) | collective-permute-done | bytes 1392 | tf_op jit(solution)/shard_map/ppermute | solution.py:22
  370.4 5.3 %collective-permute-done.59 = f32[10,34,1]{2,1,0:T(8,128)S(1)} collective-permute-done((f32[10,34,1]{2,1,0:T(8,128)S(1)}, f32[10,34,1]{2,1,0:T(8,128)S(1)}, u32[]{:S(2)}, u32[]{:S(2)}) %collective-permute-start.59) | collective-permute-done | bytes 1392 | tf_op jit(solution)/shard_map/ppermute | solution.py:19
  378.2 1.9 collective-permute-done.61
  385.2 2.0 collective-permute-start.64
  387.9 5.2 %collective-permute-done.64 = f32[10,34,1]{2,1,0:T(8,128)S(1)} collective-permute-done((f32[10,34,1]{2,1,0:T(8,128)S(1)}, f32[10,34,1]{2,1,0:T(8,128)S(1)}, u32[]{:S(2)}, u32[]{:S(2)}) %collective-permute-start.64) | collective-permute-done | bytes 1392 | tf_op jit(solution)/shard_map/ppermute | solution.py:22
  393.1 5.1 %collective-permute-done.65 = f32[10,34,1]{2,1,0:T(8,128)S(1)} collective-permute-done((f32[10,34,1]{2,1,0:T(8,128)S(1)}, f32[10,34,1]{2,1,0:T(8,128)S(1)}, u32[]{:S(2)}, u32[]{:S(2)}) %collective-permute-start.65) | collective-permute-done | bytes 1392 | tf_op jit(solution)/shard_map/ppermute | solution.py:19
  400.7 2.0 collective-permute-done.67
  410.5 4.1 collective-permute-done.70
  414.7 5.3 %collective-permute-done.71 = f32[10,34,1]{2,1,0:T(8,128)S(1)} collective-permute-done((f32[10,34,1]{2,1,0:T(8,128)S(1)}, f32[10,34,1]{2,1,0:T(8,128)S(1)}, u32[]{:S(2)}, u32[]{:S(2)}) %collective-permute-start.71) | collective-permute-done | bytes 1392 | tf_op jit(solution)/shard_map/ppermute | solution.py:19
  420.2 8.6 %fusion.17 = f32[16]{0:T(128)S(1)} fusion(f32[16,8,32,256]{3,2,1,0:T(8,128)} %param.19, f32[8,32,256,1]{2,1,0,3:T(8,128)S(1)} %bitcast.126), kind=kOutput, calls=%fused_computation.13 | convolution fusion | flops 12582912 | bytes 4456512 | tf_op jit(solution)/shard_map/dot_general | solution.py:50
  429.0 39.1 %psum.31 = f32[16]{0:T(128)S(1)} all-reduce(f32[16]{0:T(128)S(1)} %fusion.17), channel_id=1, replica_groups=mesh['gx'=2,'gy'=4,'gz'=4] {'gx','gy','gz'}, use_global_device_ids=true, to_apply=%region_8.0 | all-reduce | flops 16 | bytes 128 | tf_op jit(solution)/shard_map/psum | solution.py:91
  468.0 2.0 broadcast_select_fusion
  488.0 5.1 %multiply_add_fusion = f32[8,32,256]{2,1,0:T(8,128)} fusion(f32[8,32,256]{2,1,0:T(8,128)S(1)} %get-tuple-element.99, f32[8,32,256]{2,1,0:T(8,128)S(1)} %fusion.26, f32[]{:T(128)} %bitcast.50, f32[]{:T(128)} %sqrt.24, f32[]{:T(128)} %bitcast.49, f32[]{:T(128)} %bitcast.48, f32[]{:T(128)} %bitcast.47, f32[]{:T(128)} %bitcast.46, f32[]{:T(128)} %bitcast.45, ...), kind=kLoop, calls=%fused_computation.351 | loop fusion | flops 1048576 | bytes 1310760 | tf_op jit(solution)/shard_map/add | solution.py:109
  (194 shorter events, 94.9 us)
Async XLA Ops:
  52.8 4.2 collective-permute-start.1
  55.2 3.9 collective-permute-start
  59.1 3.1 collective-permute-start.3
  59.2 3.1 collective-permute-start.2
  62.4 7.8 %collective-permute-start.4 = (f32[10,34,1]{2,1,0:T(8,128)S(1)}, f32[10,34,1]{2,1,0:T(8,128)S(1)}, u32[]{:S(2)}, u32[]{:S(2)}) collective-permute-start(f32[10,34,1]{2,1,0:T(8,128)S(1)} %get-tuple-element.124), channel_id=1, source_target_pairs={{1,0},{2,1},{3,2},{0,3},{5,4},{6,5},{7,6},{4,7},{9,8},{10,9},{11,1... | collective-permute-start | bytes 4088 | tf_op jit(solution)/shard_map/ppermute | solution.py:22
  64.7 11.6 %collective-permute-start.5 = (f32[10,34,1]{2,1,0:T(8,128)S(1)}, f32[10,34,1]{2,1,0:T(8,128)S(1)}, u32[]{:S(2)}, u32[]{:S(2)}) collective-permute-start(f32[10,34,1]{2,1,0:T(8,128)S(1)} %get-tuple-element.125), channel_id=1, source_target_pairs={{0,1},{1,2},{2,3},{3,0},{4,5},{5,6},{6,7},{7,4},{8,9},{9,10},{10,1... | collective-permute-start | bytes 4088 | tf_op jit(solution)/shard_map/ppermute | solution.py:19
  76.6 4.0 collective-permute-start.7
  76.7 4.3 collective-permute-start.6
  81.0 3.1 collective-permute-start.9
  84.3 7.5 %collective-permute-start.10 = (f32[10,34,1]{2,1,0:T(8,128)S(1)}, f32[10,34,1]{2,1,0:T(8,128)S(1)}, u32[]{:S(2)}, u32[]{:S(2)}) collective-permute-start(f32[10,34,1]{2,1,0:T(8,128)S(1)} %get-tuple-element.122), channel_id=1, source_target_pairs={{1,0},{2,1},{3,2},{0,3},{5,4},{6,5},{7,6},{4,7},{9,8},{10,9},{11,1... | collective-permute-start | bytes 4088 | tf_op jit(solution)/shard_map/ppermute | solution.py:22
  86.4 10.8 %collective-permute-start.11 = (f32[10,34,1]{2,1,0:T(8,128)S(1)}, f32[10,34,1]{2,1,0:T(8,128)S(1)}, u32[]{:S(2)}, u32[]{:S(2)}) collective-permute-start(f32[10,34,1]{2,1,0:T(8,128)S(1)} %get-tuple-element.123), channel_id=1, source_target_pairs={{0,1},{1,2},{2,3},{3,0},{4,5},{5,6},{6,7},{7,4},{8,9},{9,10},{10,1... | collective-permute-start | bytes 4088 | tf_op jit(solution)/shard_map/ppermute | solution.py:19
  97.6 4.0 collective-permute-start.13
  99.1 3.9 collective-permute-start.12
  103.0 3.1 collective-permute-start.15
  106.4 7.9 %collective-permute-start.16 = (f32[10,34,1]{2,1,0:T(8,128)S(1)}, f32[10,34,1]{2,1,0:T(8,128)S(1)}, u32[]{:S(2)}, u32[]{:S(2)}) collective-permute-start(f32[10,34,1]{2,1,0:T(8,128)S(1)} %get-tuple-element.120), channel_id=1, source_target_pairs={{1,0},{2,1},{3,2},{0,3},{5,4},{6,5},{7,6},{4,7},{9,8},{10,9},{11,1... | collective-permute-start | bytes 4088 | tf_op jit(solution)/shard_map/ppermute | solution.py:22
  108.3 10.8 %collective-permute-start.17 = (f32[10,34,1]{2,1,0:T(8,128)S(1)}, f32[10,34,1]{2,1,0:T(8,128)S(1)}, u32[]{:S(2)}, u32[]{:S(2)}) collective-permute-start(f32[10,34,1]{2,1,0:T(8,128)S(1)} %get-tuple-element.121), channel_id=1, source_target_pairs={{0,1},{1,2},{2,3},{3,0},{4,5},{5,6},{6,7},{7,4},{8,9},{9,10},{10,1... | collective-permute-start | bytes 4088 | tf_op jit(solution)/shard_map/ppermute | solution.py:19
  119.5 4.0 collective-permute-start.19
  120.1 3.9 collective-permute-start.18
  124.1 3.1 collective-permute-start.21
  124.1 3.1 collective-permute-start.20
  127.4 7.5 %collective-permute-start.22 = (f32[10,34,1]{2,1,0:T(8,128)S(1)}, f32[10,34,1]{2,1,0:T(8,128)S(1)}, u32[]{:S(2)}, u32[]{:S(2)}) collective-permute-start(f32[10,34,1]{2,1,0:T(8,128)S(1)} %get-tuple-element.118), channel_id=1, source_target_pairs={{1,0},{2,1},{3,2},{0,3},{5,4},{6,5},{7,6},{4,7},{9,8},{10,9},{11,1... | collective-permute-start | bytes 4088 | tf_op jit(solution)/shard_map/ppermute | solution.py:22
  129.5 11.5 %collective-permute-start.23 = (f32[10,34,1]{2,1,0:T(8,128)S(1)}, f32[10,34,1]{2,1,0:T(8,128)S(1)}, u32[]{:S(2)}, u32[]{:S(2)}) collective-permute-start(f32[10,34,1]{2,1,0:T(8,128)S(1)} %get-tuple-element.119), channel_id=1, source_target_pairs={{0,1},{1,2},{2,3},{3,0},{4,5},{5,6},{6,7},{7,4},{8,9},{9,10},{10,1... | collective-permute-start | bytes 4088 | tf_op jit(solution)/shard_map/ppermute | solution.py:19
  190.2 4.2 collective-permute-start.25
  192.5 3.9 collective-permute-start.24
  196.4 3.1 collective-permute-start.27
  199.8 7.8 %collective-permute-start.28 = (f32[10,34,1]{2,1,0:T(8,128)S(1)}, f32[10,34,1]{2,1,0:T(8,128)S(1)}, u32[]{:S(2)}, u32[]{:S(2)}) collective-permute-start(f32[10,34,1]{2,1,0:T(8,128)S(1)} %get-tuple-element.116), channel_id=1, source_target_pairs={{1,0},{2,1},{3,2},{0,3},{5,4},{6,5},{7,6},{4,7},{9,8},{10,9},{11,1... | collective-permute-start | bytes 4088 | tf_op jit(solution)/shard_map/ppermute | solution.py:22
  202.1 11.5 %collective-permute-start.29 = (f32[10,34,1]{2,1,0:T(8,128)S(1)}, f32[10,34,1]{2,1,0:T(8,128)S(1)}, u32[]{:S(2)}, u32[]{:S(2)}) collective-permute-start(f32[10,34,1]{2,1,0:T(8,128)S(1)} %get-tuple-element.117), channel_id=1, source_target_pairs={{0,1},{1,2},{2,3},{3,0},{4,5},{5,6},{6,7},{7,4},{8,9},{9,10},{10,1... | collective-permute-start | bytes 4088 | tf_op jit(solution)/shard_map/ppermute | solution.py:19
  214.6 4.0 collective-permute-start.31
  214.7 4.3 collective-permute-start.30
  218.9 3.1 collective-permute-start.33
  222.3 7.7 %collective-permute-start.34 = (f32[10,34,1]{2,1,0:T(8,128)S(1)}, f32[10,34,1]{2,1,0:T(8,128)S(1)}, u32[]{:S(2)}, u32[]{:S(2)}) collective-permute-start(f32[10,34,1]{2,1,0:T(8,128)S(1)} %get-tuple-element.114), channel_id=1, source_target_pairs={{1,0},{2,1},{3,2},{0,3},{5,4},{6,5},{7,6},{4,7},{9,8},{10,9},{11,1... | collective-permute-start | bytes 4088 | tf_op jit(solution)/shard_map/ppermute | solution.py:22
  224.3 10.9 %collective-permute-start.35 = (f32[10,34,1]{2,1,0:T(8,128)S(1)}, f32[10,34,1]{2,1,0:T(8,128)S(1)}, u32[]{:S(2)}, u32[]{:S(2)}) collective-permute-start(f32[10,34,1]{2,1,0:T(8,128)S(1)} %get-tuple-element.115), channel_id=1, source_target_pairs={{0,1},{1,2},{2,3},{3,0},{4,5},{5,6},{6,7},{7,4},{8,9},{9,10},{10,1... | collective-permute-start | bytes 4088 | tf_op jit(solution)/shard_map/ppermute | solution.py:19
  235.6 4.0 collective-permute-start.37
  237.4 3.9 collective-permute-start.36
  241.3 3.1 collective-permute-start.39
  244.7 7.8 %collective-permute-start.40 = (f32[10,34,1]{2,1,0:T(8,128)S(1)}, f32[10,34,1]{2,1,0:T(8,128)S(1)}, u32[]{:S(2)}, u32[]{:S(2)}) collective-permute-start(f32[10,34,1]{2,1,0:T(8,128)S(1)} %get-tuple-element.112), channel_id=1, source_target_pairs={{1,0},{2,1},{3,2},{0,3},{5,4},{6,5},{7,6},{4,7},{9,8},{10,9},{11,1... | collective-permute-start | bytes 4088 | tf_op jit(solution)/shard_map/ppermute | solution.py:22
  246.8 11.1 %collective-permute-start.41 = (f32[10,34,1]{2,1,0:T(8,128)S(1)}, f32[10,34,1]{2,1,0:T(8,128)S(1)}, u32[]{:S(2)}, u32[]{:S(2)}) collective-permute-start(f32[10,34,1]{2,1,0:T(8,128)S(1)} %get-tuple-element.113), channel_id=1, source_target_pairs={{0,1},{1,2},{2,3},{3,0},{4,5},{5,6},{6,7},{7,4},{8,9},{9,10},{10,1... | collective-permute-start | bytes 4088 | tf_op jit(solution)/shard_map/ppermute | solution.py:19
  258.2 4.0 collective-permute-start.43
  258.7 3.9 collective-permute-start.42
  262.6 3.1 collective-permute-start.45
  266.0 8.0 %collective-permute-start.46 = (f32[10,34,1]{2,1,0:T(8,128)S(1)}, f32[10,34,1]{2,1,0:T(8,128)S(1)}, u32[]{:S(2)}, u32[]{:S(2)}) collective-permute-start(f32[10,34,1]{2,1,0:T(8,128)S(1)} %get-tuple-element.110), channel_id=1, source_target_pairs={{1,0},{2,1},{3,2},{0,3},{5,4},{6,5},{7,6},{4,7},{9,8},{10,9},{11,1... | collective-permute-start | bytes 4088 | tf_op jit(solution)/shard_map/ppermute | solution.py:22
  267.9 11.5 %collective-permute-start.47 = (f32[10,34,1]{2,1,0:T(8,128)S(1)}, f32[10,34,1]{2,1,0:T(8,128)S(1)}, u32[]{:S(2)}, u32[]{:S(2)}) collective-permute-start(f32[10,34,1]{2,1,0:T(8,128)S(1)} %get-tuple-element.111), channel_id=1, source_target_pairs={{0,1},{1,2},{2,3},{3,0},{4,5},{5,6},{6,7},{7,4},{8,9},{9,10},{10,1... | collective-permute-start | bytes 4088 | tf_op jit(solution)/shard_map/ppermute | solution.py:19
  331.5 4.2 collective-permute-start.49
  333.8 3.9 collective-permute-start.48
  337.7 3.1 collective-permute-start.51
  341.1 8.0 %collective-permute-start.52 = (f32[10,34,1]{2,1,0:T(8,128)S(1)}, f32[10,34,1]{2,1,0:T(8,128)S(1)}, u32[]{:S(2)}, u32[]{:S(2)}) collective-permute-start(f32[10,34,1]{2,1,0:T(8,128)S(1)} %get-tuple-element.108), channel_id=1, source_target_pairs={{1,0},{2,1},{3,2},{0,3},{5,4},{6,5},{7,6},{4,7},{9,8},{10,9},{11,1... | collective-permute-start | bytes 4088 | tf_op jit(solution)/shard_map/ppermute | solution.py:22
  343.4 11.3 %collective-permute-start.53 = (f32[10,34,1]{2,1,0:T(8,128)S(1)}, f32[10,34,1]{2,1,0:T(8,128)S(1)}, u32[]{:S(2)}, u32[]{:S(2)}) collective-permute-start(f32[10,34,1]{2,1,0:T(8,128)S(1)} %get-tuple-element.109), channel_id=1, source_target_pairs={{0,1},{1,2},{2,3},{3,0},{4,5},{5,6},{6,7},{7,4},{8,9},{9,10},{10,1... | collective-permute-start | bytes 4088 | tf_op jit(solution)/shard_map/ppermute | solution.py:19
  355.0 4.0 collective-permute-start.55
  355.1 4.3 collective-permute-start.54
  359.4 3.1 collective-permute-start.57
  362.8 7.7 %collective-permute-start.58 = (f32[10,34,1]{2,1,0:T(8,128)S(1)}, f32[10,34,1]{2,1,0:T(8,128)S(1)}, u32[]{:S(2)}, u32[]{:S(2)}) collective-permute-start(f32[10,34,1]{2,1,0:T(8,128)S(1)} %get-tuple-element.106), channel_id=1, source_target_pairs={{1,0},{2,1},{3,2},{0,3},{5,4},{6,5},{7,6},{4,7},{9,8},{10,9},{11,1... | collective-permute-start | bytes 4088 | tf_op jit(solution)/shard_map/ppermute | solution.py:22
  364.8 10.9 %collective-permute-start.59 = (f32[10,34,1]{2,1,0:T(8,128)S(1)}, f32[10,34,1]{2,1,0:T(8,128)S(1)}, u32[]{:S(2)}, u32[]{:S(2)}) collective-permute-start(f32[10,34,1]{2,1,0:T(8,128)S(1)} %get-tuple-element.107), channel_id=1, source_target_pairs={{0,1},{1,2},{2,3},{3,0},{4,5},{5,6},{6,7},{7,4},{8,9},{9,10},{10,1... | collective-permute-start | bytes 4088 | tf_op jit(solution)/shard_map/ppermute | solution.py:19
  376.1 4.0 collective-permute-start.61
  377.9 3.9 collective-permute-start.60
  381.8 3.1 collective-permute-start.63
  381.9 3.1 collective-permute-start.62
  385.2 7.9 %collective-permute-start.64 = (f32[10,34,1]{2,1,0:T(8,128)S(1)}, f32[10,34,1]{2,1,0:T(8,128)S(1)}, u32[]{:S(2)}, u32[]{:S(2)}) collective-permute-start(f32[10,34,1]{2,1,0:T(8,128)S(1)} %get-tuple-element.104), channel_id=1, source_target_pairs={{1,0},{2,1},{3,2},{0,3},{5,4},{6,5},{7,6},{4,7},{9,8},{10,9},{11,1... | collective-permute-start | bytes 4088 | tf_op jit(solution)/shard_map/ppermute | solution.py:22
  387.2 11.0 %collective-permute-start.65 = (f32[10,34,1]{2,1,0:T(8,128)S(1)}, f32[10,34,1]{2,1,0:T(8,128)S(1)}, u32[]{:S(2)}, u32[]{:S(2)}) collective-permute-start(f32[10,34,1]{2,1,0:T(8,128)S(1)} %get-tuple-element.105), channel_id=1, source_target_pairs={{0,1},{1,2},{2,3},{3,0},{4,5},{5,6},{6,7},{7,4},{8,9},{9,10},{10,1... | collective-permute-start | bytes 4088 | tf_op jit(solution)/shard_map/ppermute | solution.py:19
  398.6 4.1 collective-permute-start.67
  399.5 3.9 collective-permute-start.66
  403.4 3.1 collective-permute-start.69
  403.5 3.1 collective-permute-start.68
  406.8 7.9 %collective-permute-start.70 = (f32[10,34,1]{2,1,0:T(8,128)S(1)}, f32[10,34,1]{2,1,0:T(8,128)S(1)}, u32[]{:S(2)}, u32[]{:S(2)}) collective-permute-start(f32[10,34,1]{2,1,0:T(8,128)S(1)} %get-tuple-element.102), channel_id=1, source_target_pairs={{1,0},{2,1},{3,2},{0,3},{5,4},{6,5},{7,6},{4,7},{9,8},{10,9},{11,1... | collective-permute-start | bytes 4088 | tf_op jit(solution)/shard_map/ppermute | solution.py:22
  408.6 11.3 %collective-permute-start.71 = (f32[10,34,1]{2,1,0:T(8,128)S(1)}, f32[10,34,1]{2,1,0:T(8,128)S(1)}, u32[]{:S(2)}, u32[]{:S(2)}) collective-permute-start(f32[10,34,1]{2,1,0:T(8,128)S(1)} %get-tuple-element.103), channel_id=1, source_target_pairs={{0,1},{1,2},{2,3},{3,0},{4,5},{5,6},{6,7},{7,4},{8,9},{9,10},{10,1... | collective-permute-start | bytes 4088 | tf_op jit(solution)/shard_map/ppermute | solution.py:19
  (13 other events, 274.9 us)
where the time goes:
time: 502 us; the launch traced here: 494 us
  waiting for transfers between devices  181 us (36%)
  blocking collectives  159 us (32%)
  starting transfers between devices  73.7 us (15%)
  matrix products  37 us (7%)
  other arithmetic  24.6 us (5%)
  between operations  10.4 us (2%)
  local copies, waits for them, and re-layouts  8.33 us (2%)
    psum x3, blocking collectives, local(): lax.psum(local_sketch(sketch_rows, product), ('gx', 'gy', 'gz'))  117 us
    ppermute x36, waiting for transfers between devices, extended(): lax.ppermute(lax.slice_in_dim(block, block.shape[dim] - width, None, axis...  103 us
    ppermute x36, waiting for transfers between devices, extended(): lax.ppermute(lax.slice_in_dim(block, 0, width, axis=dim), axis, backward)  77.8 us
    ppermute x36, starting transfers between devices, extended(): lax.ppermute(lax.slice_in_dim(block, 0, width, axis=dim), axis, backward)  57.6 us
    psum x1, blocking collectives, local(): lax.psum(local_sketch(sketch_rows, right_side), ('gx', 'gy', 'gz'))  42 us
    dot_general x4, matrix products, local_sketch(): jnp.dot(sketch_rows, grid_field.reshape(-1), precision=HIGH, preferred_el...  31.3 us
    ppermute x36, starting transfers between devices, extended(): lax.ppermute(lax.slice_in_dim(block, block.shape[dim] - width, None, axis...  16.2 us
  transfers between devices with their start and end apart: 72, of which 59 were waited for; matrix products, arithmetic and copies ran while one was open for 1% of the time, Pallas kernels for 0%

commit v1 on v0

v1 whole, which is shorter than its diff:
```python
import functools

import jax
import jax.numpy as jnp
from jax import lax
from jax.experimental import pallas as pl
from jax.experimental.pallas import tpu as pltpu
from jax.sharding import PartitionSpec as P

SWEEPS = 3
ITERS = 3
DEPTH = SWEEPS + 1
SHIFTS = (0.75, 0.5, 0.25)
MESH = pl.DeviceIdType.MESH
LANES = 128


def small_solve(sketches):
    def dot(a, b):
        return jnp.sum(a * b, axis=0, keepdims=True)

    beta = jnp.sqrt(dot(sketches[0], sketches[0]))
    combos = [[1.0 / beta]]
    images = [sketches[0] / beta]
    hessen = []
    for it in range(ITERS):
        a = combos[it]
        b = [SHIFTS[i] * a[i] for i in range(it + 1)] + [None]
        for i in range(1, it + 2):
            b[i] = a[i - 1] if b[i] is None else b[i] + a[i - 1]
        s = b[0] * sketches[0]
        for i in range(1, it + 2):
            s = s + b[i] * sketches[i]
        c = [dot(images[i], s) for i in range(it + 1)]
        t = s
        for i in range(it + 1):
            t = t - c[i] * images[i]
            for m in range(i + 1):
                b[m] = b[m] - c[i] * combos[i][m]
        nu = jnp.sqrt(dot(t, t))
        images.append(t / nu)
        combos.append([x / nu for x in b])
        hessen.append(c + [nu])

    def vdot(a, b):
        total = a[0] * b[0]
        for i in range(1, min(len(a), len(b))):
            total = total + a[i] * b[i]
        return total

    basis, upper = [], [[None] * ITERS for _ in range(ITERS)]
    for col in range(ITERS):
        column = list(hessen[col])
        for row in range(col):
            factor = vdot(basis[row], column)
            upper[row][col] = factor
            for i in range(len(basis[row])):
                column[i] = column[i] - factor * basis[row][i]
        norm = jnp.sqrt(vdot(column, column))
        upper[col][col] = norm
        basis.append([x / norm for x in column])
    y = [None] * ITERS
    for row in reversed(range(ITERS)):
        acc = basis[row][0] * beta
        for col in range(row + 1, ITERS):
            acc = acc - upper[row][col] * y[col]
        y[row] = acc / upper[row][row]
    e = []
    for i in range(ITERS + 1):
        acc = beta if i == 0 else jnp.zeros_like(beta)
        for col in range(ITERS):
            if i <= col + 1:
                acc = acc - hessen[col][i] * y[col]
        e.append(acc)
    sol, res = [], []
    for i in range(ITERS):
        acc = y[i] * combos[i][i]
        for j in range(i + 1, ITERS):
            acc = acc + y[j] * combos[j][i]
        sol.append(acc)
    for i in range(ITERS + 1):
        acc = e[i] * combos[i][i]
        for j in range(i + 1, ITERS + 1):
            acc = acc + e[j] * combos[j][i]
        res.append(acc)
    return sol, res


def kernel(sizes, r_ref, k_ref, s_ref, sol_ref, res_ref,
           sk, ksq, dinv, basis, last, za, zb, pk,
           ysend, yrecv, zsend, zrecv, crecv, red0, red1, red2, got1, got2,
           local_sem, gsend, grecv, xsend, xrecv, rsend1, rrecv1, rsend2, rrecv2):
    nx, ny, nz = sizes
    bx, by, bz = r_ref.shape
    rows = sk.shape[0]
    X, Y, Z = nx * bx, by + 2 * DEPTH, bz + LANES
    half = X // 2
    per = LANES // DEPTH
    groups = zsend.shape[-1] // LANES
    gx, gy, gz = lax.axis_index("gx"), lax.axis_index("gy"), lax.axis_index("gz")

    def wrap(i, n):
        return lax.rem(i + n, n)

    py, qy = wrap(gy - 1, ny), wrap(gy + 1, ny)
    pz, qz = wrap(gz - 1, nz), wrap(gz + 1, nz)

    plane_peers = []
    for dx in range(nx):
        for dy in range(ny):
            if dx or dy:
                plane_peers.append((wrap(gx + dx, nx), wrap(gy + dy, ny), gz))
    z_peers = [(gx, gy, wrap(gz + d, nz)) for d in range(1, nz)]
    diagonals = [(gx, py, pz), (gx, qy, pz), (gx, py, qz), (gx, qy, qz)]

    own_s = pltpu.make_async_copy(s_ref, sk, local_sem.at[0])
    own_k = pltpu.make_async_copy(
        k_ref, ksq.at[pl.ds(0, bx), pl.ds(0, by), pl.ds(0, bz)], local_sem.at[1])
    own_r = pltpu.make_async_copy(
        r_ref, basis.at[0, pl.ds(0, bx), pl.ds(0, by), pl.ds(0, bz)], local_sem.at[2])
    own_k.start()
    own_r.start()
    own_s.start()

    barrier = pltpu.get_barrier_semaphore()
    everyone = plane_peers + z_peers + diagonals
    for peer in everyone:
        pl.semaphore_signal(barrier, inc=1, device_id=peer, device_id_type=MESH)
    pl.semaphore_wait(barrier, len(everyone))

    gathers = []
    for which, src in ((0, k_ref), (1, r_ref)):
        for i in range(1, nx):
            dst = ksq if which == 0 else basis.at[0]
            copy = pltpu.make_async_remote_copy(
                src_ref=src,
                dst_ref=dst.at[pl.ds(i * bx, bx), pl.ds(0, by), pl.ds(0, bz)],
                send_sem=gsend.at[which, i - 1], recv_sem=grecv.at[which, i - 1],
                device_id=(wrap(gx - i, nx), gy, gz), device_id_type=MESH)
            copy.start()
            gathers.append((which, copy))

    sub_low = lax.broadcasted_iota(jnp.int32, (8, bz), 0) < DEPTH
    sub_low_z = lax.broadcasted_iota(jnp.int32, (8, zsend.shape[-1]), 0) < DEPTH
    lane_by = lax.broadcasted_iota(jnp.int32, (by, LANES), 1)
    lane_y = lax.broadcasted_iota(jnp.int32, (Y, LANES), 1)

    pending = []

    def exchange_start(slot, buf):
        def pack_y(p, carry):
            low0, low1 = buf[p, 0:8, 0:bz], buf[p + half, 0:8, 0:bz]
            high0, high1 = buf[p, by - 8:by, 0:bz], buf[p + half, by - 8:by, 0:bz]
            ysend[slot, 0, p] = jnp.where(sub_low, low0, pltpu.roll(low1, DEPTH, 0))
            ysend[slot, 1, p] = jnp.where(sub_low, pltpu.roll(high0, DEPTH, 0), high1)
            return carry

        lax.fori_loop(0, half, pack_y, 0)
        copies = []

        def send(m, src, dst, peer):
            copy = pltpu.make_async_remote_copy(
                src_ref=src, dst_ref=dst, send_sem=xsend.at[slot, m], recv_sem=xrecv.at[slot, m],
                device_id=peer, device_id_type=MESH)
            copy.start()
            copies.append(copy)

        send(0, ysend.at[slot, 0], yrecv.at[slot, 0], (gx, py, gz))
        send(1, ysend.at[slot, 1], yrecv.at[slot, 1], (gx, qy, gz))
        for g in range(groups):
            def pack_z(p, carry):
                left, right = carry
                plane = g * per + p
                mine = lax.div(lane_by, DEPTH) == p
                first = pltpu.roll(buf[plane, 0:by, 0:LANES], DEPTH * p, 1)
                final = pltpu.roll(
                    buf[plane, 0:by, bz - LANES:bz], lax.rem(DEPTH * (p + 1), LANES), 1)
                return jnp.where(mine, first, left), jnp.where(mine, final, right)

            zero = jnp.zeros((by, LANES), jnp.float32)
            left, right = lax.fori_loop(0, min(per, X - g * per), pack_z, (zero, zero))
            zsend[slot, 0, :, g * LANES:(g + 1) * LANES] = left
            zsend[slot, 1, :, g * LANES:(g + 1) * LANES] = right
        send(2, zsend.at[slot, 0], zrecv.at[slot, 0], (gx, gy, pz))
        send(3, zsend.at[slot, 1], zrecv.at[slot, 1], (gx, gy, qz))
        for m, (side, row, peer) in enumerate((
                (0, 0, (gx, py, pz)), (0, by - 8, (gx, qy, pz)),
                (1, 0, (gx, py, qz)), (1, by - 8, (gx, qy, qz)))):
            send(4 + m, zsend.at[slot, side, pl.ds(row, 8)], crecv.at[slot, m], peer)
        pending.extend(copies)
        return copies

    def exchange_finish(slot, buf, copies):
        copies[0].wait_recv()
        copies[1].wait_recv()

        def unpack_y(p, carry):
            up, down = yrecv[slot, 0, p], yrecv[slot, 1, p]
            buf[p, by:Y, 0:bz] = jnp.where(sub_low, up, pltpu.roll(down, DEPTH, 0))
            buf[p + half, by:Y, 0:bz] = jnp.where(sub_low, pltpu.roll(up, DEPTH, 0), down)
            return carry

        lax.fori_loop(0, half, unpack_y, 0)
        for copy in copies[2:]:
            copy.wait_recv()
        right = jnp.concatenate(
            [zrecv[slot, 0], jnp.where(sub_low_z, crecv[slot, 0], crecv[slot, 1])], axis=0)
        left = jnp.concatenate(
            [zrecv[slot, 1], jnp.where(sub_low_z, crecv[slot, 2], crecv[slot, 3])], axis=0)
        for g in range(groups):
            right_g = right[:, g * LANES:(g + 1) * LANES]
            left_g = left[:, g * LANES:(g + 1) * LANES]

            def unpack_z(p, carry):
                high = pltpu.roll(right_g, lax.rem(LANES - DEPTH * p, LANES), 1)
                low = pltpu.roll(left_g, LANES - DEPTH - DEPTH * p, 1)
                tile = jnp.where(
                    lane_y < DEPTH, high, jnp.where(lane_y >= LANES - DEPTH, low, 0.0))
                buf[g * per + p, :, bz:Z] = tile
                return carry

            lax.fori_loop(0, min(per, X - g * per), unpack_z, 0)

    def near(z_ref, p):
        centre = z_ref[p]
        total = z_ref[lax.rem(p + X - 1, X)] + z_ref[lax.rem(p + 1, X)]
        total = total + pltpu.roll(centre, 1, 0) + pltpu.roll(centre, Y - 1, 0)
        total = total + pltpu.roll(centre, 1, 1) + pltpu.roll(centre, Z - 1, 1)
        return centre, total

    def sketch(slot, plane_of):
        def body(p, acc):
            v = plane_of(p)
            out = []
            for row in range(rows):
                prod = sk[row, p] * v
                part = prod[:, 0:LANES]
                for i in range(1, bz // LANES):
                    part = part + prod[:, i * LANES:(i + 1) * LANES]
                tile = part[0:8]
                for i in range(1, by // 8):
                    tile = tile + part[8 * i:8 * i + 8]
                out.append(acc[row] + tile)
            return tuple(out)

        acc = lax.fori_loop(0, bx, body, tuple(jnp.zeros((8, LANES), jnp.float32) for _ in range(rows)))
        for row in range(rows):
            red0[slot, pl.ds(row, 1)] = jnp.sum(acc[row], axis=0, keepdims=True)

    own_k.wait()
    for which, copy in gathers:
        if which == 0:
            copy.wait_recv()
    k_copies = exchange_start(0, ksq)
    own_r.wait()
    own_s.wait()
    sketch(0, lambda p: basis[0, p, 0:by, 0:bz])
    exchange_finish(0, ksq, k_copies)

    def invert(p, carry):
        dinv[p] = 1.0 / (6.0 + ksq[p])
        return carry

    lax.fori_loop(0, X, invert, 0)
    for which, copy in gathers:
        if which == 1:
            copy.wait_recv()

    copies = exchange_start(1, basis.at[0])
    for it in range(ITERS):
        vec = basis.at[it]
        if it:
            sketch(it, lambda p: vec[p, 0:by, 0:bz])
        exchange_finish(it + 1, vec, copies)

        def scale(p, carry):
            za[p] = vec[p] * dinv[p]
            return carry

        lax.fori_loop(0, X, scale, 0)
        src, dst = za, zb
        for sweep in range(SWEEPS):
            def jacobi(p, carry):
                centre, total = near(src, p)
                dst[p] = (vec[p] + total) * dinv[p]
                return carry

            lax.fori_loop(0, X, jacobi, 0)
            src, dst = dst, src

        def operate(p, carry):
            centre, total = near(src, p)
            inner = centre[0:by, 0:bz]
            value = (6.0 - ksq[p, 0:by, 0:bz]) * inner - total[0:by, 0:bz]
            value = value - SHIFTS[it] * vec[p, 0:by, 0:bz]
            if it == ITERS - 1:
                last[p] = value
            else:
                basis[it + 1, p, 0:by, 0:bz] = value
            return carry

        lax.fori_loop(0, bx if it == ITERS - 1 else X, operate, 0)
        if it < ITERS - 1:
            copies = exchange_start(it + 2, basis.at[it + 1])

        def keep(p, carry):
            pk[it, p] = src[p, 0:by, 0:bz]
            return carry

        lax.fori_loop(0, bx, keep, 0)
    sketch(ITERS, lambda p: last[p])

    lane_r = lax.broadcasted_iota(jnp.int32, (rows, LANES), 1)
    table = jnp.zeros((rows, LANES), jnp.float32)
    for j in range(ITERS + 1):
        table = jnp.where(lane_r == j, jnp.sum(red0[j], axis=1, keepdims=True), table)
    red1[...] = table
    for buf, got, peers, ssem, rsem, out in (
            (red1, got1, plane_peers, rsend1, rrecv1, red2), (red2, got2, z_peers, rsend2, rrecv2, None)):
        sums = []
        for m, peer in enumerate(peers):
            copy = pltpu.make_async_remote_copy(
                src_ref=buf, dst_ref=got.at[m], send_sem=ssem.at[m], recv_sem=rsem.at[m],
                device_id=peer, device_id_type=MESH)
            copy.start()
            sums.append(copy)
        total = buf[...]
        for m, copy in enumerate(sums):
            copy.wait_recv()
            total = total + got[m]
        pending.extend(sums)
        if out is not None:
            out[...] = total
    sketches = []
    for j in range(ITERS + 1):
        column = jnp.sum(jnp.where(lane_r == j, total, 0.0), axis=1, keepdims=True)
        sketches.append(jnp.broadcast_to(column, (rows, LANES)))
    sol, res = small_solve(sketches)
    wide = bz // LANES
    sol = [jnp.concatenate([c] * wide, axis=1) for c in sol]
    res = [jnp.concatenate([c] * wide, axis=1) for c in res]

    def combine(p, carry):
        acc = pk[0, p] * sol[0]
        for i in range(1, ITERS):
            acc = acc + pk[i, p] * sol[i]
        sol_ref[p] = acc
        acc = last[p] * res[ITERS]
        for i in range(ITERS):
            acc = acc + basis[i, p, 0:by, 0:bz] * res[i]
        res_ref[p] = acc
        return carry

    lax.fori_loop(0, bx, combine, 0)
    for which, copy in gathers:
        copy.wait_send()
    for copy in pending:
        copy.wait_send()


def solution(mesh):
    nx, ny, nz = mesh.shape["gx"], mesh.shape["gy"], mesh.shape["gz"]

    def local(right_side, wavenumber_sq, sketch_matrix):
        rows, bx, by, bz = sketch_matrix.shape
        X, Y, Z = nx * bx, by + 2 * DEPTH, bz + LANES
        packed = -(-X * DEPTH // LANES) * LANES
        slots = ITERS + 1
        f32 = jnp.float32
        dma = pltpu.SemaphoreType.DMA
        plane, line = nx * ny - 1, nz - 1
        return pl.pallas_call(
            functools.partial(kernel, (nx, ny, nz)),
            out_shape=(jax.ShapeDtypeStruct((bx, by, bz), f32),) * 2,
            in_specs=[pl.BlockSpec(memory_space=pl.ANY)] * 3,
            out_specs=[pl.BlockSpec(memory_space=pltpu.VMEM)] * 2,
            scratch_shapes=[
                pltpu.VMEM((rows, bx, by, bz), f32),
                pltpu.VMEM((X, Y, Z), f32),
                pltpu.VMEM((X, Y, Z), f32),
                pltpu.VMEM((ITERS, X, Y, Z), f32),
                pltpu.VMEM((bx, by, bz), f32),
                pltpu.VMEM((X, Y, Z), f32),
                pltpu.VMEM((X, Y, Z), f32),
                pltpu.VMEM((ITERS, bx, by, bz), f32),
                pltpu.VMEM((slots, 2, X // 2, 8, bz), f32),
                pltpu.VMEM((slots, 2, X // 2, 8, bz), f32),
                pltpu.VMEM((slots, 2, by, packed), f32),
                pltpu.VMEM((slots, 2, by, packed), f32),
                pltpu.VMEM((slots, 4, 8, packed), f32),
                pltpu.VMEM((slots, rows, LANES), f32),
                pltpu.VMEM((rows, LANES), f32),
                pltpu.VMEM((rows, LANES), f32),
                pltpu.VMEM((plane, rows, LANES), f32),
                pltpu.VMEM((line, rows, LANES), f32),
                dma((3,)),
                dma((2, nx - 1)), dma((2, nx - 1)),
                dma((slots, 8)), dma((slots, 8)),
                dma((plane,)), dma((plane,)),
                dma((line,)), dma((line,)),
            ],
            compiler_params=pltpu.CompilerParams(
                collective_id=0, has_side_effects=True, vmem_limit_bytes=60 * 1024 * 1024),
        )(right_side, wavenumber_sq, sketch_matrix)

    spec = P("gx", "gy", "gz")
    return jax.shard_map(
        local, mesh=mesh, in_specs=(spec, spec, P(None, "gx", "gy", "gz")),
        out_specs=(spec, spec), check_vma=False)
```

time: 502 us -> 73.1 us (0.15); the launches traced: 494 us -> 72.9 us
  waiting for transfers between devices: 181 us -> 0 us
  blocking collectives: 159 us -> 0 us
  starting transfers between devices: 73.7 us -> 0 us
  Pallas kernels: 0 us -> 68.9 us
  matrix products: 37 us -> 0 us
  other arithmetic: 24.6 us -> 0 us
  between operations: 10.4 us -> 0.64 us
    ppermute x72 -> x0, waiting for transfers between devices: 181 us -> none  [the longest x36 103 us: extended(): lax.ppermute(lax.slice_in_dim(block, block.shape[dim] - width, None, axis...]
    psum x4 -> x0, blocking collectives: 159 us -> none  [the longest x3 117 us: local(): lax.psum(local_sketch(sketch_rows, product), ('gx', 'gy', 'gz'))]
    ppermute x72 -> x0, starting transfers between devices: 73.7 us -> none  [the longest x36 57.6 us: extended(): lax.ppermute(lax.slice_in_dim(block, 0, width, axis=dim), axis, backward)]
    pallas_call x0 -> x1, Pallas kernels: none -> 68.9 us  [local(): pl.pallas_call(functools.partial(kernel, (nx, ny, nz)), out_shape=(jax.Sh...]
    dot_general x9 -> x0, matrix products: 37 us -> none  [the longest x4 31.3 us: local_sketch(): jnp.dot(sketch_rows, grid_field.reshape(-1), precision=HIGH, preferred_el...]
    add x11 -> x0, other arithmetic: 9.45 us -> none  [the longest x1 5.14 us: local(): residual = residual + vectors[member] * leftover[member]]
    reduce_sum x8 -> x0, other arithmetic: 8.76 us -> none  [the longest x3 3.16 us: solve_small(): diag_term = jnp.sqrt(jnp.sum(column * column))]
  transfers between devices with their start and end apart: 72 -> 0, of which waited for: 59 -> 0; matrix products, arithmetic and copies ran while one was open for 1% -> 0% of each run, Pallas kernels for 0% -> 0%
where the time goes in v1:
time: 73.1 us; the launch traced here: 72.9 us
  Pallas kernels  68.9 us (94%)
  local copies, waits for them, and re-layouts  3.34 us (5%)
    pallas_call x1, Pallas kernels, local(): pl.pallas_call(functools.partial(kernel, (nx, ny, nz)), out_shape=(jax.Sh...  68.9 us
    unnamed x2, local copies, waits for them, and re-layouts  3.34 us

profile of v1, /device:TPU:0, one launch (start us, length us, event | category | flops | bytes accessed | tf_op | source)
XLA Modules:
  0.0 72.9 jit_solution(7032309236874327594)
XLA Ops:
  0.6 68.9 %shard_map.50 = (f32[8,32,256]{2,1,0:T(8,128)}, f32[8,32,256]{2,1,0:T(8,128)}) custom-call(f32[8,32,256]{2,1,0:T(8,128)} %r_ref.1, f32[8,32,256]{2,1,0:T(8,128)} %k_ref.1, f32[16,8,32,256]{3,2,1,0:T(8,128)} %s_ref.1), custom_call_target="tpu_custom_call" | custom-call | tf_op jit(solution)/shard_map/pallas_call | solution.py:372
  69.5 1.7 %copy.7 = f32[8,32,256]{2,1,0:T(8,128)} copy(f32[8,32,256]{2,1,0:T(8,128)} %get-tuple-element.4) | data formatting | bytes 524288
  71.2 1.7 %copy.8 = f32[8,32,256]{2,1,0:T(8,128)} copy(f32[8,32,256]{2,1,0:T(8,128)} %get-tuple-element.5) | data formatting | bytes 524288

commit v2 on v1

--- a/solution.py
+++ b/solution.py
@@ -13,6 +13,18 @@
 SHIFTS = (0.75, 0.5, 0.25)
 MESH = pl.DeviceIdType.MESH
 LANES = 128
+
+
+def planes(count, step, body, carry):
+    while count % step:
+        step //= 2
+
+    def group(at, carry):
+        for i in range(step):
+            carry = body(at * step + i, carry)
+        return carry
+
+    return lax.fori_loop(0, count // step, group, carry)
 
 
 def small_solve(sketches):
@@ -155,7 +167,7 @@
             ysend[slot, 1, p] = jnp.where(sub_low, pltpu.roll(high0, DEPTH, 0), high1)
             return carry
 
-        lax.fori_loop(0, half, pack_y, 0)
+        planes(half, 4, pack_y, 0)
         copies = []
 
         def send(m, src, dst, peer):
@@ -178,7 +190,7 @@
                 return jnp.where(mine, first, left), jnp.where(mine, final, right)
 
             zero = jnp.zeros((by, LANES), jnp.float32)
-            left, right = lax.fori_loop(0, min(per, X - g * per), pack_z, (zero, zero))
+            left, right = planes(min(per, X - g * per), 8, pack_z, (zero, zero))
             zsend[slot, 0, :, g * LANES:(g + 1) * LANES] = left
             zsend[slot, 1, :, g * LANES:(g + 1) * LANES] = right
         send(2, zsend.at[slot, 0], zrecv.at[slot, 0], (gx, gy, pz))
@@ -200,7 +212,7 @@
             buf[p + half, by:Y, 0:bz] = jnp.where(sub_low, pltpu.roll(up, DEPTH, 0), down)
             return carry
 
-        lax.fori_loop(0, half, unpack_y, 0)
+        planes(half, 4, unpack_y, 0)
         for copy in copies[2:]:
             copy.wait_recv()
         right = jnp.concatenate(
@@ -219,7 +231,7 @@
                 buf[g * per + p, :, bz:Z] = tile
                 return carry
 
-            lax.fori_loop(0, min(per, X - g * per), unpack_z, 0)
+            planes(min(per, X - g * per), 8, unpack_z, 0)
 
     def near(z_ref, p):
         centre = z_ref[p]
@@ -255,18 +267,17 @@
     own_r.wait()
     own_s.wait()
     sketch(0, lambda p: basis[0, p, 0:by, 0:bz])
+    for which, copy in gathers:
+        if which == 1:
+            copy.wait_recv()
+    copies = exchange_start(1, basis.at[0])
     exchange_finish(0, ksq, k_copies)
 
     def invert(p, carry):
         dinv[p] = 1.0 / (6.0 + ksq[p])
         return carry
 
-    lax.fori_loop(0, X, invert, 0)
-    for which, copy in gathers:
-        if which == 1:
-            copy.wait_recv()
-
-    copies = exchange_start(1, basis.at[0])
+    planes(X, 4, invert, 0)
     for it in range(ITERS):
         vec = basis.at[it]
         if it:
@@ -277,15 +288,24 @@
             za[p] = vec[p] * dinv[p]
             return carry
 
-        lax.fori_loop(0, X, scale, 0)
+        planes(X, 4, scale, 0)
         src, dst = za, zb
         for sweep in range(SWEEPS):
-            def jacobi(p, carry):
-                centre, total = near(src, p)
-                dst[p] = (vec[p] + total) * dinv[p]
+            reach = SWEEPS - sweep
+            shrunk = it == ITERS - 1 and bx + 2 * reach < X
+            begin, count = (X - reach, bx + 2 * reach) if shrunk else (0, X)
+
+            def jacobi(at, carry):
+                where = [lax.rem(begin + 2 * at + i, X) for i in range(2)]
+                values = []
+                for p in where:
+                    centre, total = near(src, p)
+                    values.append((vec[p] + total) * dinv[p])
+                for p, value in zip(where, values):
+                    dst[p] = value
                 return carry
 
-            lax.fori_loop(0, X, jacobi, 0)
+            lax.fori_loop(0, count // 2, jacobi, 0)
             src, dst = dst, src
 
         def operate(p, carry):
@@ -299,7 +319,7 @@
                 basis[it + 1, p, 0:by, 0:bz] = value
             return carry
 
-        lax.fori_loop(0, bx if it == ITERS - 1 else X, operate, 0)
+        planes(bx if it == ITERS - 1 else X, 2, operate, 0)
         if it < ITERS - 1:
             copies = exchange_start(it + 2, basis.at[it + 1])
 
@@ -307,7 +327,7 @@
             pk[it, p] = src[p, 0:by, 0:bz]
             return carry
 
-        lax.fori_loop(0, bx, keep, 0)
+        planes(bx, 4, keep, 0)
     sketch(ITERS, lambda p: last[p])
 
     lane_r = lax.broadcasted_iota(jnp.int32, (rows, LANES), 1)
@@ -351,11 +371,16 @@
         res_ref[p] = acc
         return carry
 
-    lax.fori_loop(0, bx, combine, 0)
+    planes(bx, 2, combine, 0)
     for which, copy in gathers:
         copy.wait_send()
     for copy in pending:
         copy.wait_send()
+
+
+def write_out(a_ref, b_ref, sol_ref, res_ref):
+    sol_ref[...] = a_ref[...]
+    res_ref[...] = b_ref[...]
 
 
 def solution(mesh):
@@ -369,7 +394,7 @@
         f32 = jnp.float32
         dma = pltpu.SemaphoreType.DMA
         plane, line = nx * ny - 1, nz - 1
-        return pl.pallas_call(
+        found = pl.pallas_call(
             functools.partial(kernel, (nx, ny, nz)),
             out_shape=(jax.ShapeDtypeStruct((bx, by, bz), f32),) * 2,
             in_specs=[pl.BlockSpec(memory_space=pl.ANY)] * 3,
@@ -402,6 +427,12 @@
             compiler_params=pltpu.CompilerParams(
                 collective_id=0, has_side_effects=True, vmem_limit_bytes=60 * 1024 * 1024),
         )(right_side, wavenumber_sq, sketch_matrix)
+        return pl.pallas_call(
+            write_out,
+            out_shape=(jax.ShapeDtypeStruct((bx, by, bz), f32),) * 2,
+            in_specs=[pl.BlockSpec(memory_space=pltpu.VMEM)] * 2,
+            out_specs=[pl.BlockSpec(memory_space=pltpu.VMEM)] * 2,
+        )(*found)
 
     spec = P("gx", "gy", "gz")
     return jax.shard_map(

time: 73.1 us -> 57.3 us (0.78)
  Pallas kernels: 68.9 us -> 56.5 us
  local copies, waits for them, and re-layouts: 3.34 us -> 0 us
    pallas_call x1, Pallas kernels: 68.9 us -> 54.6 us  [local(): pl.pallas_call(functools.partial(kernel, (nx, ny, nz)), out_shape=(jax.Sh...]
    unnamed x2 -> x0, local copies, waits for them, and re-layouts: 3.34 us -> none
    pallas_call x0 -> x1, Pallas kernels: none -> 1.84 us  [local(): pl.pallas_call(write_out, out_shape=(jax.ShapeDtypeStruct((bx, by, bz), f...]
where the time goes in v2:
time: 57.3 us; the launch traced here: 57.1 us
  Pallas kernels  56.5 us (99%)
  between operations  0.64 us (1%)
    pallas_call x1, Pallas kernels, local(): pl.pallas_call(functools.partial(kernel, (nx, ny, nz)), out_shape=(jax.Sh...  54.6 us
    pallas_call x1, Pallas kernels, local(): pl.pallas_call(write_out, out_shape=(jax.ShapeDtypeStruct((bx, by, bz), f...  1.84 us

profile of v2, /device:TPU:0, one launch (start us, length us, event | category | flops | bytes accessed | tf_op | source)
XLA Modules:
  0.0 57.1 jit_solution(12847413556577659705)
XLA Ops:
  0.6 54.6 %shard_map.50 = (f32[8,32,256]{2,1,0:T(8,128)}, f32[8,32,256]{2,1,0:T(8,128)}) custom-call(f32[8,32,256]{2,1,0:T(8,128)} %r_ref.1, f32[8,32,256]{2,1,0:T(8,128)} %k_ref.1, f32[16,8,32,256]{3,2,1,0:T(8,128)} %s_ref.1), custom_call_target="tpu_custom_call" | custom-call | tf_op jit(solution)/shard_map/pallas_call | solution.py:397
  55.3 1.8 %shard_map.51 = (f32[8,32,256]{2,1,0:T(8,128)}, f32[8,32,256]{2,1,0:T(8,128)}) custom-call(f32[8,32,256]{2,1,0:T(8,128)} %get-tuple-element.4.a_ref, f32[8,32,256]{2,1,0:T(8,128)} %get-tuple-element.5.b_ref), custom_call_target="tpu_custom_call" | custom-call | tf_op jit(solution)/shard_map/pallas_call | solution.py:430

commit v3 on v2

--- a/solution.py
+++ b/solution.py
@@ -255,7 +255,7 @@
                 out.append(acc[row] + tile)
             return tuple(out)
 
-        acc = lax.fori_loop(0, bx, body, tuple(jnp.zeros((8, LANES), jnp.float32) for _ in range(rows)))
+        acc = planes(bx, 2, body, tuple(jnp.zeros((8, LANES), jnp.float32) for _ in range(rows)))
         for row in range(rows):
             red0[slot, pl.ds(row, 1)] = jnp.sum(acc[row], axis=0, keepdims=True)
 
@@ -295,8 +295,10 @@
             shrunk = it == ITERS - 1 and bx + 2 * reach < X
             begin, count = (X - reach, bx + 2 * reach) if shrunk else (0, X)
 
+            step = 4 if count % 4 == 0 else 2
+
             def jacobi(at, carry):
-                where = [lax.rem(begin + 2 * at + i, X) for i in range(2)]
+                where = [lax.rem(begin + step * at + i, X) for i in range(step)]
                 values = []
                 for p in where:
                     centre, total = near(src, p)
@@ -305,21 +307,25 @@
                     dst[p] = value
                 return carry
 
-            lax.fori_loop(0, count // 2, jacobi, 0)
+            lax.fori_loop(0, count // step, jacobi, 0)
             src, dst = dst, src
 
-        def operate(p, carry):
-            centre, total = near(src, p)
-            inner = centre[0:by, 0:bz]
-            value = (6.0 - ksq[p, 0:by, 0:bz]) * inner - total[0:by, 0:bz]
-            value = value - SHIFTS[it] * vec[p, 0:by, 0:bz]
-            if it == ITERS - 1:
-                last[p] = value
-            else:
-                basis[it + 1, p, 0:by, 0:bz] = value
+        def operate(at, carry):
+            values = []
+            for i in range(4):
+                p = 4 * at + i
+                centre, total = near(src, p)
+                inner = centre[0:by, 0:bz]
+                value = (6.0 - ksq[p, 0:by, 0:bz]) * inner - total[0:by, 0:bz]
+                values.append(value - SHIFTS[it] * vec[p, 0:by, 0:bz])
+            for i, value in enumerate(values):
+                if it == ITERS - 1:
+                    last[4 * at + i] = value
+                else:
+                    basis[it + 1, 4 * at + i, 0:by, 0:bz] = value
             return carry
 
-        planes(bx if it == ITERS - 1 else X, 2, operate, 0)
+        lax.fori_loop(0, (bx if it == ITERS - 1 else X) // 4, operate, 0)
         if it < ITERS - 1:
             copies = exchange_start(it + 2, basis.at[it + 1])
 
@@ -330,10 +336,14 @@
         planes(bx, 4, keep, 0)
     sketch(ITERS, lambda p: last[p])
 
-    lane_r = lax.broadcasted_iota(jnp.int32, (rows, LANES), 1)
-    table = jnp.zeros((rows, LANES), jnp.float32)
+    lane_r = lax.broadcasted_iota(jnp.int32, (8, LANES), 1)
+    table = jnp.zeros((8, LANES), jnp.float32)
+    parts = rows // 8
     for j in range(ITERS + 1):
-        table = jnp.where(lane_r == j, jnp.sum(red0[j], axis=1, keepdims=True), table)
+        for h in range(parts):
+            table = jnp.where(
+                lane_r == j * parts + h,
+                jnp.sum(red0[j, pl.ds(8 * h, 8)], axis=1, keepdims=True), table)
     red1[...] = table
     for buf, got, peers, ssem, rsem, out in (
             (red1, got1, plane_peers, rsend1, rrecv1, red2), (red2, got2, z_peers, rsend2, rrecv2, None)):
@@ -353,8 +363,10 @@
             out[...] = total
     sketches = []
     for j in range(ITERS + 1):
-        column = jnp.sum(jnp.where(lane_r == j, total, 0.0), axis=1, keepdims=True)
-        sketches.append(jnp.broadcast_to(column, (rows, LANES)))
+        sketches.append(jnp.concatenate([
+            jnp.broadcast_to(jnp.sum(
+                jnp.where(lane_r == j * parts + h, total, 0.0), axis=1, keepdims=True), (8, LANES))
+            for h in range(parts)], axis=0))
     sol, res = small_solve(sketches)
     wide = bz // LANES
     sol = [jnp.concatenate([c] * wide, axis=1) for c in sol]
@@ -414,10 +426,10 @@
                 pltpu.VMEM((slots, 2, by, packed), f32),
                 pltpu.VMEM((slots, 4, 8, packed), f32),
                 pltpu.VMEM((slots, rows, LANES), f32),
-                pltpu.VMEM((rows, LANES), f32),
-                pltpu.VMEM((rows, LANES), f32),
-                pltpu.VMEM((plane, rows, LANES), f32),
-                pltpu.VMEM((line, rows, LANES), f32),
+                pltpu.VMEM((8, LANES), f32),
+                pltpu.VMEM((8, LANES), f32),
+                pltpu.VMEM((plane, 8, LANES), f32),
+                pltpu.VMEM((line, 8, LANES), f32),
                 dma((3,)),
                 dma((2, nx - 1)), dma((2, nx - 1)),
                 dma((slots, 8)), dma((slots, 8)),

time: 57.3 us -> 54.5 us (0.951)
  Pallas kernels: 56.5 us -> 53.8 us
    pallas_call x1, Pallas kernels: 54.6 us -> 51.9 us  [local(): pl.pallas_call(functools.partial(kernel, (nx, ny, nz)), out_shape=(jax.Sh...]
where the time goes in v3:
time: 54.5 us; the launch traced here: 54.4 us
  Pallas kernels  53.8 us (99%)
  between operations  0.64 us (1%)
    pallas_call x1, Pallas kernels, local(): pl.pallas_call(functools.partial(kernel, (nx, ny, nz)), out_shape=(jax.Sh...  51.9 us
    pallas_call x1, Pallas kernels, local(): pl.pallas_call(write_out, out_shape=(jax.ShapeDtypeStruct((bx, by, bz), f...  1.84 us

profile of v3, /device:TPU:0, one launch (start us, length us, event | category | flops | bytes accessed | tf_op | source)
XLA Modules:
  0.0 54.4 jit_solution(17454933020650202690)
XLA Ops:
  0.6 51.9 %shard_map.50 = (f32[8,32,256]{2,1,0:T(8,128)}, f32[8,32,256]{2,1,0:T(8,128)}) custom-call(f32[8,32,256]{2,1,0:T(8,128)} %r_ref.1, f32[8,32,256]{2,1,0:T(8,128)} %k_ref.1, f32[16,8,32,256]{3,2,1,0:T(8,128)} %s_ref.1), custom_call_target="tpu_custom_call" | custom-call | tf_op jit(solution)/shard_map/pallas_call | solution.py:409
  52.6 1.8 %shard_map.51 = (f32[8,32,256]{2,1,0:T(8,128)}, f32[8,32,256]{2,1,0:T(8,128)}) custom-call(f32[8,32,256]{2,1,0:T(8,128)} %get-tuple-element.4.a_ref, f32[8,32,256]{2,1,0:T(8,128)} %get-tuple-element.5.b_ref), custom_call_target="tpu_custom_call" | custom-call | tf_op jit(solution)/shard_map/pallas_call | solution.py:442

commit v4 on v3

--- a/solution.py
+++ b/solution.py
@@ -295,16 +295,13 @@
             shrunk = it == ITERS - 1 and bx + 2 * reach < X
             begin, count = (X - reach, bx + 2 * reach) if shrunk else (0, X)
 
-            step = 4 if count % 4 == 0 else 2
+            step = max(n for n in range(1, 9) if count % n == 0)
 
             def jacobi(at, carry):
                 where = [lax.rem(begin + step * at + i, X) for i in range(step)]
-                values = []
                 for p in where:
                     centre, total = near(src, p)
-                    values.append((vec[p] + total) * dinv[p])
-                for p, value in zip(where, values):
-                    dst[p] = value
+                    dst[p] = (vec[p] + total) * dinv[p]
                 return carry
 
             lax.fori_loop(0, count // step, jacobi, 0)

time: 54.5 us -> 53.2 us (0.976)
  Pallas kernels: 53.8 us -> 52.4 us
    pallas_call x1, Pallas kernels: 51.9 us -> 50.6 us  [local(): pl.pallas_call(functools.partial(kernel, (nx, ny, nz)), out_shape=(jax.Sh...]
where the time goes in v4:
time: 53.2 us; the launch traced here: 53.1 us
  Pallas kernels  52.4 us (98%)
  between operations  0.64 us (1%)
    pallas_call x1, Pallas kernels, local(): pl.pallas_call(functools.partial(kernel, (nx, ny, nz)), out_shape=(jax.Sh...  50.6 us
    pallas_call x1, Pallas kernels, local(): pl.pallas_call(write_out, out_shape=(jax.ShapeDtypeStruct((bx, by, bz), f...  1.84 us

profile of v4, /device:TPU:0, one launch (start us, length us, event | category | flops | bytes accessed | tf_op | source)
XLA Modules:
  0.0 53.1 jit_solution(580820681833475154)
XLA Ops:
  0.6 50.6 %shard_map.50 = (f32[8,32,256]{2,1,0:T(8,128)}, f32[8,32,256]{2,1,0:T(8,128)}) custom-call(f32[8,32,256]{2,1,0:T(8,128)} %r_ref.1, f32[8,32,256]{2,1,0:T(8,128)} %k_ref.1, f32[16,8,32,256]{3,2,1,0:T(8,128)} %s_ref.1), custom_call_target="tpu_custom_call" | custom-call | tf_op jit(solution)/shard_map/pallas_call | solution.py:406
  51.2 1.8 %shard_map.51 = (f32[8,32,256]{2,1,0:T(8,128)}, f32[8,32,256]{2,1,0:T(8,128)}) custom-call(f32[8,32,256]{2,1,0:T(8,128)} %get-tuple-element.4.a_ref, f32[8,32,256]{2,1,0:T(8,128)} %get-tuple-element.5.b_ref), custom_call_target="tpu_custom_call" | custom-call | tf_op jit(solution)/shard_map/pallas_call | solution.py:439

commit v5 on v4

--- a/solution.py
+++ b/solution.py
@@ -99,9 +99,10 @@
 
 
 def kernel(sizes, r_ref, k_ref, s_ref, sol_ref, res_ref,
-           sk, ksq, dinv, basis, last, za, zb, pk,
+           sk, ksq, dinv, base0, base1, base2, last, za, zb, pk,
            ysend, yrecv, zsend, zrecv, crecv, red0, red1, red2, got1, got2,
            local_sem, gsend, grecv, xsend, xrecv, rsend1, rrecv1, rsend2, rrecv2):
+    basis = (base0, base1, base2)
     nx, ny, nz = sizes
     bx, by, bz = r_ref.shape
     rows = sk.shape[0]
@@ -129,7 +130,7 @@
     own_k = pltpu.make_async_copy(
         k_ref, ksq.at[pl.ds(0, bx), pl.ds(0, by), pl.ds(0, bz)], local_sem.at[1])
     own_r = pltpu.make_async_copy(
-        r_ref, basis.at[0, pl.ds(0, bx), pl.ds(0, by), pl.ds(0, bz)], local_sem.at[2])
+        r_ref, basis[0].at[pl.ds(0, bx), pl.ds(0, by), pl.ds(0, bz)], local_sem.at[2])
     own_k.start()
     own_r.start()
     own_s.start()
@@ -143,7 +144,7 @@
     gathers = []
     for which, src in ((0, k_ref), (1, r_ref)):
         for i in range(1, nx):
-            dst = ksq if which == 0 else basis.at[0]
+            dst = ksq if which == 0 else basis[0]
             copy = pltpu.make_async_remote_copy(
                 src_ref=src,
                 dst_ref=dst.at[pl.ds(i * bx, bx), pl.ds(0, by), pl.ds(0, bz)],
@@ -266,11 +267,11 @@
     k_copies = exchange_start(0, ksq)
     own_r.wait()
     own_s.wait()
-    sketch(0, lambda p: basis[0, p, 0:by, 0:bz])
+    sketch(0, lambda p: basis[0][p, 0:by, 0:bz])
     for which, copy in gathers:
         if which == 1:
             copy.wait_recv()
-    copies = exchange_start(1, basis.at[0])
+    copies = exchange_start(1, basis[0])
     exchange_finish(0, ksq, k_copies)
 
     def invert(p, carry):
@@ -279,7 +280,7 @@
 
     planes(X, 4, invert, 0)
     for it in range(ITERS):
-        vec = basis.at[it]
+        vec = basis[it]
         if it:
             sketch(it, lambda p: vec[p, 0:by, 0:bz])
         exchange_finish(it + 1, vec, copies)
@@ -307,24 +308,20 @@
             lax.fori_loop(0, count // step, jacobi, 0)
             src, dst = dst, src
 
-        def operate(at, carry):
-            values = []
-            for i in range(4):
-                p = 4 * at + i
-                centre, total = near(src, p)
-                inner = centre[0:by, 0:bz]
-                value = (6.0 - ksq[p, 0:by, 0:bz]) * inner - total[0:by, 0:bz]
-                values.append(value - SHIFTS[it] * vec[p, 0:by, 0:bz])
-            for i, value in enumerate(values):
-                if it == ITERS - 1:
-                    last[4 * at + i] = value
-                else:
-                    basis[it + 1, 4 * at + i, 0:by, 0:bz] = value
+        def operate(p, carry):
+            centre, total = near(src, p)
+            inner = centre[0:by, 0:bz]
+            value = (6.0 - ksq[p, 0:by, 0:bz]) * inner - total[0:by, 0:bz]
+            value = value - SHIFTS[it] * vec[p, 0:by, 0:bz]
+            if it == ITERS - 1:
+                last[p] = value
+            else:
+                basis[it + 1][p, 0:by, 0:bz] = value
             return carry
 
-        lax.fori_loop(0, (bx if it == ITERS - 1 else X) // 4, operate, 0)
+        planes(bx if it == ITERS - 1 else X, 8, operate, 0)
         if it < ITERS - 1:
-            copies = exchange_start(it + 2, basis.at[it + 1])
+            copies = exchange_start(it + 2, basis[it + 1])
 
         def keep(p, carry):
             pk[it, p] = src[p, 0:by, 0:bz]
@@ -376,7 +373,7 @@
         sol_ref[p] = acc
         acc = last[p] * res[ITERS]
         for i in range(ITERS):
-            acc = acc + basis[i, p, 0:by, 0:bz] * res[i]
+            acc = acc + basis[i][p, 0:by, 0:bz] * res[i]
         res_ref[p] = acc
         return carry
 
@@ -412,7 +409,9 @@
                 pltpu.VMEM((rows, bx, by, bz), f32),
                 pltpu.VMEM((X, Y, Z), f32),
                 pltpu.VMEM((X, Y, Z), f32),
-                pltpu.VMEM((ITERS, X, Y, Z), f32),
+                pltpu.VMEM((X, Y, Z), f32),
+                pltpu.VMEM((X, Y, Z), f32),
+                pltpu.VMEM((X, Y, Z), f32),
                 pltpu.VMEM((bx, by, bz), f32),
                 pltpu.VMEM((X, Y, Z), f32),
                 pltpu.VMEM((X, Y, Z), f32),

time: 53.2 us -> 52.9 us (level)
  no operation moved by 1% of the time
where the time goes in v5:
time: 52.9 us; the launch traced here: 52.7 us
  Pallas kernels  52.1 us (98%)
  between operations  0.64 us (1%)
    pallas_call x1, Pallas kernels, local(): pl.pallas_call(functools.partial(kernel, (nx, ny, nz)), out_shape=(jax.Sh...  50.2 us
    pallas_call x1, Pallas kernels, local(): pl.pallas_call(write_out, out_shape=(jax.ShapeDtypeStruct((bx, by, bz), f...  1.84 us

profile of v5, /device:TPU:0, one launch (start us, length us, event | category | flops | bytes accessed | tf_op | source)
XLA Modules:
  0.0 52.7 jit_solution(11135878930276658164)
XLA Ops:
  0.6 50.2 %shard_map.50 = (f32[8,32,256]{2,1,0:T(8,128)}, f32[8,32,256]{2,1,0:T(8,128)}) custom-call(f32[8,32,256]{2,1,0:T(8,128)} %r_ref.1, f32[8,32,256]{2,1,0:T(8,128)} %k_ref.1, f32[16,8,32,256]{3,2,1,0:T(8,128)} %s_ref.1), custom_call_target="tpu_custom_call" | custom-call | tf_op jit(solution)/shard_map/pallas_call | solution.py:403
  50.9 1.8 %shard_map.51 = (f32[8,32,256]{2,1,0:T(8,128)}, f32[8,32,256]{2,1,0:T(8,128)}) custom-call(f32[8,32,256]{2,1,0:T(8,128)} %get-tuple-element.4.a_ref, f32[8,32,256]{2,1,0:T(8,128)} %get-tuple-element.5.b_ref), custom_call_target="tpu_custom_call" | custom-call | tf_op jit(solution)/shard_map/pallas_call | solution.py:438
